TPU v7x, 32 devices: a whole 2x2x4 slice. The times are simulated.
32 devices in a mesh: seq: 8 (over y, x, core), chan: 4 (over z).
Axes of the slice: x: 2, y: 2, z: 4, core: 2. Of those that a mesh axis runs over, the one named last changes fastest.
Arguments:
- q_in: bfloat16 [1024, 4096], P('seq', 'chan'), may hold values from -6 to 6
- k_in: bfloat16 [1024, 4096], P('seq', 'chan'), may hold values from -6 to 6
- v_in: bfloat16 [1024, 4096], P('seq', 'chan'), may hold values from -6 to 6
- short_filters: float32 [3, 3, 4096], P(None, None, 'chan'), may hold values from -3.5 to 3.5
- long_filter: float32 [4, 1024, 1024], P('chan', 'seq'), may hold values from -8 to 8
- out_weight: bfloat16 [4096, 4096], P('chan'), may hold values from -0.09375 to 0.09375
- out_grad: bfloat16 [1024, 4096], P('seq', 'chan'), may hold values from -0.059814453 to 0.059814453
Outputs:
- operator_out: bfloat16 [1024, 4096], P('seq', 'chan')
- filter_grad: float32 [4, 1024, 1024], P('chan', 'seq')
All inputs are finite; a program needn't handle non-finite values.
Results may differ from a plain program's by a relative error of at most 0.0058.
Values may be sent and summed in bfloat16 or wider, within the bound.
A program may use at most 64 MiB of HBM per device.

v0:
```python
import functools
import math

import jax
import jax.numpy as jnp
from jax import lax
from jax.experimental import pallas as pl
from jax.experimental.pallas import tpu as pltpu
from jax.sharding import PartitionSpec as P

HIGHEST = lax.Precision.HIGHEST


def shifted(value, axis, steps):
    count = lax.axis_size(axis)
    leading, last = (max(0, -steps), min(count, count - steps))
    return lax.ppermute(value, axis, [(source, source + steps) for source in range(leading, last)])


def angle_table(rows, cols, modulus):
    first = jnp.arange(rows, dtype=jnp.int32)[:, None]
    second = jnp.arange(cols, dtype=jnp.int32)[None, :]
    phase = (first * second % modulus).astype(jnp.float32) * (2.0 * math.pi / modulus)
    return (jnp.cos(phase), jnp.sin(phase))


def spectrum(signal, rows_p, cols_q):
    cos_p, sin_p = angle_table(rows_p // 2, rows_p, rows_p)
    first_re = jnp.einsum("cnq,nk->ckq", signal, cos_p, precision=HIGHEST)
    first_im = -jnp.einsum("cnq,nk->ckq", signal, sin_p, precision=HIGHEST)
    cos_t, sin_t = angle_table(rows_p, cols_q, rows_p * cols_q)
    turn_re = first_re * cos_t + first_im * sin_t
    turn_im = first_im * cos_t - first_re * sin_t
    cos_q, sin_q = angle_table(cols_q, cols_q, cols_q)
    out_re = jnp.einsum("ckq,qm->ckm", turn_re, cos_q, precision=HIGHEST) + jnp.einsum(
        "ckq,qm->ckm", turn_im, sin_q, precision=HIGHEST
    )
    out_im = jnp.einsum("ckq,qm->ckm", turn_im, cos_q, precision=HIGHEST) - jnp.einsum(
        "ckq,qm->ckm", turn_re, sin_q, precision=HIGHEST
    )
    return (out_re, out_im)


def signal_back(spec_re, spec_im, rows_p, cols_q):
    cos_q, sin_q = angle_table(cols_q, cols_q, cols_q)
    mid_re = jnp.einsum("ckm,mq->ckq", spec_re, cos_q, precision=HIGHEST) - jnp.einsum(
        "ckm,mq->ckq", spec_im, sin_q, precision=HIGHEST
    )
    mid_im = jnp.einsum("ckm,mq->ckq", spec_re, sin_q, precision=HIGHEST) + jnp.einsum(
        "ckm,mq->ckq", spec_im, cos_q, precision=HIGHEST
    )
    cos_t, sin_t = angle_table(rows_p, cols_q, rows_p * cols_q)
    turn_re = mid_re * cos_t - mid_im * sin_t
    turn_im = mid_re * sin_t + mid_im * cos_t
    cos_p, sin_p = angle_table(rows_p, rows_p // 2, rows_p)
    real_part = jnp.einsum("ckq,kn->cnq", turn_re, cos_p, precision=HIGHEST) - jnp.einsum(
        "ckq,kn->cnq", turn_im, sin_p, precision=HIGHEST
    )
    return real_part / (rows_p * cols_q)


def regroup(blocked):
    return lax.all_to_all(blocked, "seq", split_axis=0, concat_axis=1, tiled=True)


def on_device_by_spectrum(q_in, k_in, v_in, short_filters, long_filter, out_weight, out_grad):
    tokens, group_w = q_in.shape
    taps = short_filters.shape[1]
    streams = jnp.stack((q_in, k_in, v_in))
    before = shifted(streams[:, tokens - (taps - 1) :, :], "seq", 1)
    extended = jnp.concatenate((before, streams), axis=1).astype(jnp.float32)
    conv = short_filters[:, 0, None, :] * extended[:, taps - 1 : taps - 1 + tokens, :]
    for lag in range(1, taps):
        conv = (
            conv
            + short_filters[:, lag, None, :]
            * extended[:, taps - 1 - lag : taps - 1 - lag + tokens, :]
        )
    q_conv = conv[0]
    gated_t = (conv[1] * conv[2]).astype(jnp.bfloat16).T
    channels = long_filter.shape[1]
    length = long_filter.shape[2]
    cols_q = length // tokens
    rows_p = 2 * tokens
    filters = long_filter.reshape(channels, tokens, cols_q)
    z_chan = regroup(gated_t)
    z_re, z_im = spectrum(
        z_chan.astype(jnp.float32).reshape(channels, tokens, cols_q), rows_p, cols_q
    )
    h_re, h_im = spectrum(filters, rows_p, cols_q)
    y_chan = signal_back(z_re * h_re - z_im * h_im, z_re * h_im + z_im * h_re, rows_p, cols_q)
    y_chan = y_chan.reshape(channels, length).astype(jnp.bfloat16)
    y_tok = lax.all_to_all(y_chan, "seq", split_axis=1, concat_axis=0, tiled=True)
    operator_out = (q_conv * y_tok.T.astype(jnp.float32)).astype(jnp.bfloat16)
    grad_gate = jnp.einsum(
        "tw,iw->ti",
        lax.all_gather(out_grad, "chan", axis=1, tiled=True),
        out_weight,
        preferred_element_type=jnp.float32,
    )
    dy_chan = regroup((grad_gate * q_conv).astype(jnp.bfloat16).T)
    d_re, d_im = spectrum(
        dy_chan.astype(jnp.float32).reshape(channels, tokens, cols_q), rows_p, cols_q
    )
    filter_grad = signal_back(z_re * d_re + z_im * d_im, z_re * d_im - z_im * d_re, rows_p, cols_q)
    return (operator_out, filter_grad.reshape(1, channels, length))


MESH = pl.DeviceIdType.MESH
BLOCK = 128
CHUNKS = 4
F32 = jnp.float32
BF16 = jnp.bfloat16


def rows_at(start, size):
    return pl.ds(pl.multiple_of(start, size), size)


def kernel(
    q_hbm, k_hbm, v_hbm, taps_hbm, filt_hbm, weight_hbm, grad_hbm,
    out_ref, fgrad_ref,
    streams, halo, taps, filt, weight, grads,
    q_t, g_send, g_recv, g_wide, toep, h_pad, y_tiles, y_send, y_recv,
    acc, d_send, d_recv, d_pad, f_tiles,
    load_sem, halo_ssem, halo_rsem, gather_ssem, gather_rsem, fwd_ssem,
    g_ssem, g_rsem, y_ssem, y_rsem, d_ssem, d_rsem,
):
    n = g_recv.shape[0]
    me, c = lax.axis_index("seq"), lax.axis_index("chan")
    streams_hbm = (q_hbm, k_hbm, v_hbm)
    cols = grads.shape[2] // CHUNKS

    loads = [pltpu.make_async_copy(ref, streams.at[s], load_sem.at[s]) for s, ref in enumerate(streams_hbm)]
    loads.append(pltpu.make_async_copy(taps_hbm, taps, load_sem.at[3]))
    own_grad = pltpu.make_async_copy(grad_hbm, grads.at[c], load_sem.at[4])
    weight_load = pltpu.make_async_copy(weight_hbm, weight, load_sem.at[5])
    filt_loads = [
        pltpu.make_async_copy(filt_hbm.at[0, :, pl.ds(a * BLOCK, BLOCK)], filt.at[a], load_sem.at[6 + a])
        for a in range(n)
    ]
    for copy in (*loads, own_grad, *filt_loads, weight_load):
        copy.start()

    barrier = pltpu.get_barrier_semaphore()
    for r in range(1, n):
        pl.semaphore_signal(barrier, inc=1, device_id=(lax.rem(me + r, n), c), device_id_type=MESH)
    for r in range(1, 4):
        pl.semaphore_signal(barrier, inc=1, device_id=(me, lax.rem(c + r, 4)), device_id_type=MESH)
    pl.semaphore_wait(barrier, n - 1 + 3)

    nxt = lax.rem(me + 1, n)
    halo_copies = [
        pltpu.make_async_remote_copy(
            src_ref=ref.at[pl.ds(BLOCK - 16, 16), :], dst_ref=halo.at[s],
            send_sem=halo_ssem.at[s], recv_sem=halo_rsem.at[s],
            device_id=(nxt, c), device_id_type=MESH,
        )
        for s, ref in enumerate(streams_hbm)
    ]

    @pl.when(me < n - 1)
    def _():
        for copy in halo_copies:
            copy.start()

    @pl.when(me == 0)
    def _():
        halo[...] = jnp.zeros_like(halo)

    partner = c + 1 - 2 * lax.rem(c, 2)
    half = c // 2
    near = 2 - half
    far = 3 - 3 * half
    middle = jnp.logical_or(c == 1, c == 2)

    def gather_copy(block, chunk, src, dst_chan, ssem):
        return pltpu.make_async_remote_copy(
            src_ref=src, dst_ref=grads.at[block, :, pl.ds(chunk * cols, cols)],
            send_sem=ssem, recv_sem=gather_rsem.at[block, chunk],
            device_id=(me, dst_chan), device_id_type=MESH,
        )

    own_sends = []
    for chunk in range(CHUNKS):
        src = grad_hbm.at[:, pl.ds(chunk * cols, cols)]
        own_sends.append(gather_copy(c, chunk, src, partner, gather_ssem.at[0, chunk]))
        own_sends.append(gather_copy(c, chunk, src, near, gather_ssem.at[1, chunk]))
    for copy in own_sends:
        copy.start()

    def forward_copy(which, block, chunk):
        src = grads.at[block, :, pl.ds(chunk * cols, cols)]
        return gather_copy(block, chunk, src, partner, fwd_ssem.at[which, chunk])

    def forward(chunk):
        @pl.when(middle)
        def _():
            for which, block in enumerate((near, far)):
                copy = forward_copy(which, block, chunk)
                copy.wait_recv()
                copy.start()

    for copy in loads:
        copy.wait()

    @pl.when(me > 0)
    def _():
        for copy in halo_copies:
            copy.wait_recv()

    row = lax.broadcasted_iota(jnp.int32, (BLOCK, BLOCK), 0)
    lane = lax.broadcasted_iota(jnp.int32, (BLOCK, BLOCK), 1)
    flip = jnp.where(row + lane == BLOCK - 1, 1.0, 0.0).astype(BF16)

    def exchange(send_ref, recv_ref, ssem, rsem, r):
        return pltpu.make_async_remote_copy(
            src_ref=send_ref.at[lax.rem(me + r, n)], dst_ref=recv_ref.at[me],
            send_sem=ssem.at[r], recv_sem=rsem.at[r],
            device_id=(lax.rem(me + r, n), c), device_id_type=MESH,
        )

    @pl.loop(1, n + 1)
    def _(r):
        p = lax.rem(me + r, n)
        here = rows_at(p * BLOCK, BLOCK)
        conv = []
        for s in range(3):
            value = streams[s, :, here].astype(F32)
            tail = halo[s, :, here].astype(F32)
            total = taps[s, 0:1, here] * value
            one = jnp.where(row == 0, tail[15:16, :], pltpu.roll(value, 1, 0))
            total = total + taps[s, 1:2, here] * one
            two = pltpu.roll(value, 2, 0)
            two = jnp.where(row == 0, tail[14:15, :], jnp.where(row == 1, tail[15:16, :], two))
            conv.append(total + taps[s, 2:3, here] * two)
        q_t[here, :] = conv[0].T
        gated = (conv[1] * conv[2]).astype(BF16).astype(F32)
        turned = jnp.dot(gated.T.astype(BF16), flip, preferred_element_type=F32)
        g_send[p] = turned.astype(BF16)

        @pl.when(r < n)
        def _():
            exchange(g_send, g_recv, g_ssem, g_rsem, r).start()

        @pl.when(r == n)
        def _():
            g_recv[me] = turned.astype(BF16)

    h_pad[...] = jnp.zeros_like(h_pad)
    d_pad[...] = jnp.zeros_like(d_pad)
    for a in range(n):
        filt_loads[a].wait()
        value = filt[a]
        high = value.astype(BF16)
        low = (value - high.astype(F32)).astype(BF16)
        turned = jnp.dot(high, flip, preferred_element_type=F32) + jnp.dot(low, flip, preferred_element_type=F32)
        h_pad[pl.ds(n + a, BLOCK, stride=2 * n), :] = turned

    forward(0)
    for r in range(1, n):
        exchange(g_send, g_recv, g_ssem, g_rsem, r).wait_recv()
    g_wide[...] = g_recv[...].astype(F32)

    def channel(d):
        rolled = None
        for u in range(n):
            before = rolled
            source = jnp.broadcast_to(g_wide[u, pl.ds(d, 1), :], (BLOCK, BLOCK))
            rolled = pltpu.roll(source, 1, 1, stride=1, stride_axis=0)
            other = jnp.zeros_like(rolled) if before is None else before
            toep[d, u * BLOCK : (u + 1) * BLOCK, :] = jnp.where(lane <= row, rolled, other).astype(BF16)
        left = jnp.concatenate([h_pad[pl.ds(d * 2 * n + n - u, n), :] for u in range(n)], axis=1)
        high = left.astype(BF16).astype(F32)
        both = jnp.concatenate([high, left - high], axis=0).astype(BF16)
        result = jnp.dot(both, toep[d], preferred_element_type=F32)
        y_tiles[rows_at(d * n, n), :] = result[:n] + result[n:]

    def channels(first, last):
        @pl.loop(first // 2, last // 2)
        def _(pair):
            channel(pair * 2)
            channel(pair * 2 + 1)

    forward(1)
    channels(0, 32)
    forward(2)
    channels(32, 64)
    forward(3)
    channels(64, BLOCK)

    for u in range(n):
        y_send[u] = y_tiles[pl.ds(u, BLOCK, stride=n), :].astype(BF16)
    for r in range(1, n):
        exchange(y_send, y_recv, y_ssem, y_rsem, r).start()
    y_recv[me] = y_send[me]

    weight_load.wait()
    own_grad.wait()
    for at, block in enumerate((c, partner, near, far)):
        if at:
            @pl.when(jnp.logical_or(jnp.logical_not(middle), at == 1))
            def _():
                for chunk in range(CHUNKS):
                    gather_copy(block, chunk, grad_hbm.at[:, pl.ds(chunk * cols, cols)], partner, gather_ssem.at[0, chunk]).wait_recv()

        wide = grads.shape[2]

        @pl.loop(0, 4)
        def _(part):
            size = acc.shape[0] // 4
            here = rows_at(part * size, size)
            term = lax.dot_general(
                weight[here, rows_at(block * wide, wide)], grads[block],
                (((1,), (1,)), ((), ())), preferred_element_type=F32,
            )
            acc[here, :] = term if at == 0 else acc[here, :] + term

    for r in range(1, n + 1):
        p = lax.rem(me + r, n)
        here = rows_at(p * BLOCK, BLOCK)
        value = (acc[here, :] * q_t[here, :]).astype(BF16)
        if r < n:
            d_send[p] = value
            exchange(d_send, d_recv, d_ssem, d_rsem, r).start()
        else:
            d_recv[me] = value

    for r in range(1, n):
        exchange(y_send, y_recv, y_ssem, y_rsem, r).wait_recv()

    @pl.loop(0, n)
    def _(p):
        here = rows_at(p * BLOCK, BLOCK)
        y = jnp.dot(y_recv[p], flip, preferred_element_type=F32)
        out_ref[:, here] = (q_t[here, :] * y).T.astype(BF16)

    for r in range(1, n):
        exchange(d_send, d_recv, d_ssem, d_rsem, r).wait_recv()
    for u in range(n):
        d_pad[pl.ds(u, BLOCK, stride=2 * n), :] = d_recv[u].astype(F32)

    @pl.loop(0, BLOCK // 4)
    def _(four):
        for i in range(4):
            d = four * 4 + i
            left = jnp.concatenate([d_pad[pl.ds(d * 2 * n + u, n), :] for u in range(n)], axis=1)
            f_tiles[rows_at(d * n, n), :] = jnp.dot(left.astype(BF16), toep[d], preferred_element_type=F32)

    for s in range(n):
        fgrad_ref[0, :, s * BLOCK : (s + 1) * BLOCK] = f_tiles[pl.ds(s, BLOCK, stride=n), :]

    @pl.when(me < n - 1)
    def _():
        for copy in halo_copies:
            copy.wait_send()

    for copy in own_sends:
        copy.wait_send()

    @pl.when(middle)
    def _():
        for chunk in range(CHUNKS):
            for which, block in enumerate((near, far)):
                forward_copy(which, block, chunk).wait_send()

    for r in range(1, n):
        exchange(g_send, g_recv, g_ssem, g_rsem, r).wait_send()
        exchange(y_send, y_recv, y_ssem, y_rsem, r).wait_send()
        exchange(d_send, d_recv, d_ssem, d_rsem, r).wait_send()


def on_device(q_in, k_in, v_in, short_filters, long_filter, out_weight, out_grad):
    tokens, group_w = q_in.shape
    taps = short_filters.shape[1]
    channels, length = long_filter.shape[1:]
    n, chans = lax.axis_size("seq"), lax.axis_size("chan")
    fits = (tokens, channels, n, chans, taps, length) == (BLOCK, BLOCK, 8, 4, 3, 8 * BLOCK)
    if not fits or out_weight.shape != (n * BLOCK, chans * group_w):
        return on_device_by_spectrum(q_in, k_in, v_in, short_filters, long_filter, out_weight, out_grad)
    dma = pltpu.SemaphoreType.DMA
    blocks = (n, BLOCK, BLOCK)
    return pl.pallas_call(
        kernel,
        out_shape=(
            jax.ShapeDtypeStruct(q_in.shape, BF16),
            jax.ShapeDtypeStruct(long_filter.shape, F32),
        ),
        in_specs=[pl.BlockSpec(memory_space=pl.ANY)] * 7,
        out_specs=[pl.BlockSpec(memory_space=pltpu.VMEM)] * 2,
        scratch_shapes=[
            pltpu.VMEM((3, tokens, group_w), BF16),
            pltpu.VMEM((3, 16, group_w), BF16),
            pltpu.VMEM(short_filters.shape, F32),
            pltpu.VMEM(blocks, F32),
            pltpu.VMEM(out_weight.shape, BF16),
            pltpu.VMEM((chans, tokens, group_w), BF16),
            pltpu.VMEM((group_w, tokens), F32),
            pltpu.VMEM(blocks, BF16),
            pltpu.VMEM(blocks, BF16),
            pltpu.VMEM(blocks, F32),
            pltpu.VMEM((channels, length, BLOCK), BF16),
            pltpu.VMEM((channels * 2 * n, BLOCK), F32),
            pltpu.VMEM((channels * n, BLOCK), F32),
            pltpu.VMEM(blocks, BF16),
            pltpu.VMEM(blocks, BF16),
            pltpu.VMEM((group_w, tokens), F32),
            pltpu.VMEM(blocks, BF16),
            pltpu.VMEM(blocks, BF16),
            pltpu.VMEM((channels * 2 * n, BLOCK), F32),
            pltpu.VMEM((channels * n, BLOCK), F32),
            dma((6 + n,)),
            dma((3,)),
            dma((3,)),
            dma((2, CHUNKS)),
            dma((chans, CHUNKS)),
            dma((2, CHUNKS)),
            dma((n,)),
            dma((n,)),
            dma((n,)),
            dma((n,)),
            dma((n,)),
            dma((n,)),
        ],
        compiler_params=pltpu.CompilerParams(
            collective_id=0, has_side_effects=True, vmem_limit_bytes=60 * 1024 * 1024
        ),
    )(q_in, k_in, v_in, short_filters, long_filter, out_weight, out_grad)


def solution(mesh):
    in_specs = (
        P("seq", "chan"),
        P("seq", "chan"),
        P("seq", "chan"),
        P(None, None, "chan"),
        P("chan", "seq", None),
        P("chan", None),
        P("seq", "chan"),
    )
    out_specs = (P("seq", "chan"), P("chan", "seq", None))
    return jax.shard_map(
        on_device, mesh=mesh, in_specs=in_specs, out_specs=out_specs, check_vma=False
    )
```

profile of v0, /device:TPU:0, one launch (start us, length us, event | category | flops | bytes accessed | tf_op | source)
XLA Modules:
  0.0 63.1 jit_solution(7852530544556210857)
XLA Ops:
  0.6 58.9 %shard_map.86 = (bf16[128,1024]{1,0:T(8,128)(2,1)}, f32[1,128,1024]{2,1,0:T(8,128)}) custom-call(bf16[128,1024]{1,0:T(8,128)(2,1)} %q_hbm.1, bf16[128,1024]{1,0:T(8,128)(2,1)} %k_hbm.1, bf16[128,1024]{1,0:T(8,128)(2,1)} %v_hbm.1, f32[3,3,1024]{2,1,0:T(4,128)} %taps_hbm.1, f32[1,128,1024]{2,1,0:T(8,128)} %filt_hbm.1, bf16[1024,4096]{1,0:T(8,128)(2,1)} %weight_hbm.1, ...), custom_call_target="tpu_custom_call" | custom-call | tf_op jit(solution)/shard_map/pallas_call | solution.py:383
  59.5 1.7 %copy.11 = bf16[128,1024]{1,0:T(8,128)(2,1)} copy(bf16[128,1024]{1,0:T(8,128)(2,1)} %get-tuple-element.4) | data formatting | bytes 524288
  61.2 1.9 %copy.12 = f32[1,128,1024]{2,1,0:T(8,128)} copy(f32[1,128,1024]{2,1,0:T(8,128)} %get-tuple-element.5) | data formatting | bytes 1048576
where the time goes:
time: 63.3 us; the launch traced here: 63.1 us
  Pallas kernels  58.9 us (93%)
  local copies, waits for them, and re-layouts  3.55 us (6%)
  between operations  0.64 us (1%)
    pallas_call x1, Pallas kernels, on_device(): pl.pallas_call(kernel, out_shape=(jax.ShapeDtypeStruct(q_in.shape, BF16),...  58.9 us
    unnamed x2, local copies, waits for them, and re-layouts  3.55 us

commit v1 on v0

--- a/solution.py
+++ b/solution.py
@@ -262,42 +262,43 @@
         exchange(g_send, g_recv, g_ssem, g_rsem, r).wait_recv()
     g_wide[...] = g_recv[...].astype(F32)
 
-    def channel(d):
-        rolled = None
-        for u in range(n):
-            before = rolled
-            source = jnp.broadcast_to(g_wide[u, pl.ds(d, 1), :], (BLOCK, BLOCK))
-            rolled = pltpu.roll(source, 1, 1, stride=1, stride_axis=0)
-            other = jnp.zeros_like(rolled) if before is None else before
-            toep[d, u * BLOCK : (u + 1) * BLOCK, :] = jnp.where(lane <= row, rolled, other).astype(BF16)
-        left = jnp.concatenate([h_pad[pl.ds(d * 2 * n + n - u, n), :] for u in range(n)], axis=1)
-        high = left.astype(BF16).astype(F32)
-        both = jnp.concatenate([high, left - high], axis=0).astype(BF16)
-        result = jnp.dot(both, toep[d], preferred_element_type=F32)
-        y_tiles[rows_at(d * n, n), :] = result[:n] + result[n:]
-
-    def channels(first, last):
-        @pl.loop(first // 2, last // 2)
+    lane16 = lax.broadcasted_iota(jnp.int32, (16, BLOCK), 1)
+    row16 = lax.broadcasted_iota(jnp.int32, (16, BLOCK), 0)
+    keep = [lane16 <= row16 + 16 * k for k in range(BLOCK // 16)]
+
+    def build(pair):
+        for side in range(2):
+            first = []
+            for u in range(n):
+                source = jnp.broadcast_to(g_wide[u, pl.ds(pair * 2 + side, 1), :], (16, BLOCK))
+                first.append(pltpu.roll(source, 1, 1, stride=1, stride_axis=0).astype(BF16))
+            for k in range(BLOCK // 16):
+                other = jnp.zeros_like(first[0])
+                for u in range(n):
+                    turned = pltpu.roll(first[u], 16 * k, 1) if k else first[u]
+                    at = u * BLOCK + 16 * k
+                    toep[pair, at : at + 16, side * BLOCK : (side + 1) * BLOCK] = jnp.where(keep[k], turned, other)
+                    other = turned
+
+    def convolve(pair):
+        rows = []
+        for side in range(2):
+            at = (pair * 2 + side) * 2 * n + n
+            left = jnp.concatenate([h_pad[pl.ds(at - u, n), :] for u in range(n)], axis=1)
+            high = left.astype(BF16).astype(F32)
+            rows += [high, left - high]
+        both = jnp.concatenate(rows, axis=0).astype(BF16)
+        result = jnp.dot(both, toep[pair], preferred_element_type=F32)
+        y_tiles[rows_at(pair * 2 * n, n), :] = result[:n, :BLOCK] + result[n : 2 * n, :BLOCK]
+        y_tiles[rows_at(pair * 2 * n + n, n), :] = result[2 * n : 3 * n, BLOCK:] + result[3 * n :, BLOCK:]
+
+    def pairs(first, last):
+        @pl.loop(first, last)
         def _(pair):
-            channel(pair * 2)
-            channel(pair * 2 + 1)
-
-    forward(1)
-    channels(0, 32)
-    forward(2)
-    channels(32, 64)
-    forward(3)
-    channels(64, BLOCK)
-
-    for u in range(n):
-        y_send[u] = y_tiles[pl.ds(u, BLOCK, stride=n), :].astype(BF16)
-    for r in range(1, n):
-        exchange(y_send, y_recv, y_ssem, y_rsem, r).start()
-    y_recv[me] = y_send[me]
-
-    weight_load.wait()
-    own_grad.wait()
-    for at, block in enumerate((c, partner, near, far)):
+            convolve(pair - 1)
+            build(pair)
+
+    def add_block(at, block):
         if at:
             @pl.when(jnp.logical_or(jnp.logical_not(middle), at == 1))
             def _():
@@ -316,6 +317,19 @@
             )
             acc[here, :] = term if at == 0 else acc[here, :] + term
 
+    forward(1)
+    build(0)
+    pairs(1, 16)
+    forward(2)
+    pairs(16, 32)
+    forward(3)
+    weight_load.wait()
+    own_grad.wait()
+    add_block(0, c)
+    add_block(1, partner)
+    pairs(32, 44)
+    add_block(2, near)
+    add_block(3, far)
     for r in range(1, n + 1):
         p = lax.rem(me + r, n)
         here = rows_at(p * BLOCK, BLOCK)
@@ -325,6 +339,35 @@
             exchange(d_send, d_recv, d_ssem, d_rsem, r).start()
         else:
             d_recv[me] = value
+    pairs(44, BLOCK // 2)
+    convolve(BLOCK // 2 - 1)
+
+    for u in range(n):
+        y_send[u] = y_tiles[pl.ds(u, BLOCK, stride=n), :].astype(BF16)
+    for r in range(1, n):
+        exchange(y_send, y_recv, y_ssem, y_rsem, r).start()
+    y_recv[me] = y_send[me]
+
+    for r in range(1, n):
+        exchange(d_send, d_recv, d_ssem, d_rsem, r).wait_recv()
+    for u in range(n):
+        d_pad[pl.ds(u, BLOCK, stride=2 * n), :] = d_recv[u].astype(F32)
+
+    @pl.loop(0, BLOCK // 4)
+    def _(two):
+        for i in range(2):
+            pair = two * 2 + i
+            rows = []
+            for side in range(2):
+                at = (pair * 2 + side) * 2 * n
+                rows.append(jnp.concatenate([d_pad[pl.ds(at + u, n), :] for u in range(n)], axis=1))
+            both = jnp.concatenate(rows, axis=0).astype(BF16)
+            result = jnp.dot(both, toep[pair], preferred_element_type=F32)
+            f_tiles[rows_at(pair * 2 * n, n), :] = result[:n, :BLOCK]
+            f_tiles[rows_at(pair * 2 * n + n, n), :] = result[n:, BLOCK:]
+
+    for s in range(n):
+        fgrad_ref[0, :, s * BLOCK : (s + 1) * BLOCK] = f_tiles[pl.ds(s, BLOCK, stride=n), :]
 
     for r in range(1, n):
         exchange(y_send, y_recv, y_ssem, y_rsem, r).wait_recv()
@@ -334,21 +377,6 @@
         here = rows_at(p * BLOCK, BLOCK)
         y = jnp.dot(y_recv[p], flip, preferred_element_type=F32)
         out_ref[:, here] = (q_t[here, :] * y).T.astype(BF16)
-
-    for r in range(1, n):
-        exchange(d_send, d_recv, d_ssem, d_rsem, r).wait_recv()
-    for u in range(n):
-        d_pad[pl.ds(u, BLOCK, stride=2 * n), :] = d_recv[u].astype(F32)
-
-    @pl.loop(0, BLOCK // 4)
-    def _(four):
-        for i in range(4):
-            d = four * 4 + i
-            left = jnp.concatenate([d_pad[pl.ds(d * 2 * n + u, n), :] for u in range(n)], axis=1)
-            f_tiles[rows_at(d * n, n), :] = jnp.dot(left.astype(BF16), toep[d], preferred_element_type=F32)
-
-    for s in range(n):
-        fgrad_ref[0, :, s * BLOCK : (s + 1) * BLOCK] = f_tiles[pl.ds(s, BLOCK, stride=n), :]
 
     @pl.when(me < n - 1)
     def _():
@@ -399,7 +427,7 @@
             pltpu.VMEM(blocks, BF16),
             pltpu.VMEM(blocks, BF16),
             pltpu.VMEM(blocks, F32),
-            pltpu.VMEM((channels, length, BLOCK), BF16),
+            pltpu.VMEM((channels // 2, length, 2 * BLOCK), BF16),
             pltpu.VMEM((channels * 2 * n, BLOCK), F32),
             pltpu.VMEM((channels * n, BLOCK), F32),
             pltpu.VMEM(blocks, BF16),

time: 63.3 us -> 56 us (0.88)
  Pallas kernels: 58.9 us -> 51.6 us
    pallas_call x1, Pallas kernels: 58.9 us -> 51.6 us  [on_device(): pl.pallas_call(kernel, out_shape=(jax.ShapeDtypeStruct(q_in.shape, BF16),...]
where the time goes in v1:
time: 56 us; the launch traced here: 55.8 us
  Pallas kernels  51.6 us (92%)
  local copies, waits for them, and re-layouts  3.55 us (6%)
  between operations  0.64 us (1%)
    pallas_call x1, Pallas kernels, on_device(): pl.pallas_call(kernel, out_shape=(jax.ShapeDtypeStruct(q_in.shape, BF16),...  51.6 us
    unnamed x2, local copies, waits for them, and re-layouts  3.55 us

profile of v1, /device:TPU:0, one launch (start us, length us, event | category | flops | bytes accessed | tf_op | source)
XLA Modules:
  0.0 55.8 jit_solution(17447794087041256214)
XLA Ops:
  0.6 51.6 %shard_map.86 = (bf16[128,1024]{1,0:T(8,128)(2,1)}, f32[1,128,1024]{2,1,0:T(8,128)}) custom-call(bf16[128,1024]{1,0:T(8,128)(2,1)} %q_hbm.1, bf16[128,1024]{1,0:T(8,128)(2,1)} %k_hbm.1, bf16[128,1024]{1,0:T(8,128)(2,1)} %v_hbm.1, f32[3,3,1024]{2,1,0:T(4,128)} %taps_hbm.1, f32[1,128,1024]{2,1,0:T(8,128)} %filt_hbm.1, bf16[1024,4096]{1,0:T(8,128)(2,1)} %weight_hbm.1, ...), custom_call_target="tpu_custom_call" | custom-call | tf_op jit(solution)/shard_map/pallas_call | solution.py:411
  52.2 1.7 %copy.11 = bf16[128,1024]{1,0:T(8,128)(2,1)} copy(bf16[128,1024]{1,0:T(8,128)(2,1)} %get-tuple-element.4) | data formatting | bytes 524288
  53.9 1.9 %copy.12 = f32[1,128,1024]{2,1,0:T(8,128)} copy(f32[1,128,1024]{2,1,0:T(8,128)} %get-tuple-element.5) | data formatting | bytes 1048576

commit v2 on v1

--- a/solution.py
+++ b/solution.py
@@ -109,6 +109,7 @@
 MESH = pl.DeviceIdType.MESH
 BLOCK = 128
 CHUNKS = 4
+GROUP = 8
 F32 = jnp.float32
 BF16 = jnp.bfloat16
 
@@ -121,8 +122,8 @@
     q_hbm, k_hbm, v_hbm, taps_hbm, filt_hbm, weight_hbm, grad_hbm,
     out_ref, fgrad_ref,
     streams, halo, taps, filt, weight, grads,
-    q_t, g_send, g_recv, g_wide, toep, h_pad, y_tiles, y_send, y_recv,
-    acc, d_send, d_recv, d_pad, f_tiles,
+    q_t, g_send, g_recv, g_wide, toep, h_pad, h_left, y_tiles, y_send, y_recv,
+    acc, d_send, d_recv, d_pad, d_even, d_odd, f_tiles,
     load_sem, halo_ssem, halo_rsem, gather_ssem, gather_rsem, fwd_ssem,
     g_ssem, g_rsem, y_ssem, y_rsem, d_ssem, d_rsem,
 ):
@@ -201,6 +202,48 @@
                 copy.wait_recv()
                 copy.start()
 
+    row = lax.broadcasted_iota(jnp.int32, (BLOCK, BLOCK), 0)
+    lane = lax.broadcasted_iota(jnp.int32, (BLOCK, BLOCK), 1)
+    flip = jnp.where(row + lane == BLOCK - 1, 1.0, 0.0).astype(BF16)
+
+    def lay_out(pad, blocks):
+        pad[...] = jnp.zeros_like(pad)
+        for r in range(4):
+            turned = [pltpu.roll(x, BLOCK - 32 * r, 1) if r else x for x in blocks]
+            for a in range(n):
+                value = turned[a]
+                if r:
+                    after = turned[a + 1] if a + 1 < n else jnp.zeros_like(value)
+                    value = jnp.where(lane < BLOCK - 32 * r, value, after)
+                pad[r, pl.ds(a, BLOCK, stride=2 * n), :] = value
+
+    def left_rows(pad, channel, r, u):
+        at = channel * 2 * n
+        return jnp.concatenate([pad[r, pl.ds(at + u, n), :], pad[r + 1, pl.ds(at + u, n), :]], axis=0)
+
+    blocks = []
+    for a in reversed(range(n)):
+        filt_loads[a].wait()
+        value = filt[a]
+        high = value.astype(BF16)
+        low = (value - high.astype(F32)).astype(BF16)
+        blocks.append(
+            jnp.dot(high, flip, preferred_element_type=F32) + jnp.dot(low, flip, preferred_element_type=F32)
+        )
+    lay_out(h_pad, blocks)
+
+    @pl.loop(0, BLOCK // GROUP)
+    def _(group):
+        for j in range(GROUP):
+            for r in (0, 2):
+                for u in range(n):
+                    value = left_rows(h_pad, group * GROUP + j, r, u)
+                    high = value.astype(BF16)
+                    at = 32 * j + 8 * r
+                    here = slice(u * BLOCK, (u + 1) * BLOCK)
+                    h_left[group, at : at + 16, here] = high
+                    h_left[group, 256 + at : 256 + at + 16, here] = (value - high.astype(F32)).astype(BF16)
+
     for copy in loads:
         copy.wait()
 
@@ -208,10 +251,6 @@
     def _():
         for copy in halo_copies:
             copy.wait_recv()
-
-    row = lax.broadcasted_iota(jnp.int32, (BLOCK, BLOCK), 0)
-    lane = lax.broadcasted_iota(jnp.int32, (BLOCK, BLOCK), 1)
-    flip = jnp.where(row + lane == BLOCK - 1, 1.0, 0.0).astype(BF16)
 
     def exchange(send_ref, recv_ref, ssem, rsem, r):
         return pltpu.make_async_remote_copy(
@@ -220,8 +259,7 @@
             device_id=(lax.rem(me + r, n), c), device_id_type=MESH,
         )
 
-    @pl.loop(1, n + 1)
-    def _(r):
+    for r in range(1, n + 1):
         p = lax.rem(me + r, n)
         here = rows_at(p * BLOCK, BLOCK)
         conv = []
@@ -235,27 +273,12 @@
             two = jnp.where(row == 0, tail[14:15, :], jnp.where(row == 1, tail[15:16, :], two))
             conv.append(total + taps[s, 2:3, here] * two)
         q_t[here, :] = conv[0].T
-        gated = (conv[1] * conv[2]).astype(BF16).astype(F32)
-        turned = jnp.dot(gated.T.astype(BF16), flip, preferred_element_type=F32)
-        g_send[p] = turned.astype(BF16)
-
-        @pl.when(r < n)
-        def _():
+        gated = (conv[1] * conv[2]).T.astype(BF16)
+        if r < n:
+            g_send[p] = gated
             exchange(g_send, g_recv, g_ssem, g_rsem, r).start()
-
-        @pl.when(r == n)
-        def _():
-            g_recv[me] = turned.astype(BF16)
-
-    h_pad[...] = jnp.zeros_like(h_pad)
-    d_pad[...] = jnp.zeros_like(d_pad)
-    for a in range(n):
-        filt_loads[a].wait()
-        value = filt[a]
-        high = value.astype(BF16)
-        low = (value - high.astype(F32)).astype(BF16)
-        turned = jnp.dot(high, flip, preferred_element_type=F32) + jnp.dot(low, flip, preferred_element_type=F32)
-        h_pad[pl.ds(n + a, BLOCK, stride=2 * n), :] = turned
+        else:
+            g_recv[me] = gated
 
     forward(0)
     for r in range(1, n):
@@ -264,39 +287,44 @@
 
     lane16 = lax.broadcasted_iota(jnp.int32, (16, BLOCK), 1)
     row16 = lax.broadcasted_iota(jnp.int32, (16, BLOCK), 0)
-    keep = [lane16 <= row16 + 16 * k for k in range(BLOCK // 16)]
-
-    def build(pair):
-        for side in range(2):
-            first = []
+    keep = [lane16 >= row16 + 16 * k for k in range(2)]
+    strip = lax.broadcasted_iota(jnp.int32, (n, BLOCK), 1) // 32
+
+    def build(group):
+        for j in range(GROUP):
+            other = [jnp.zeros((16, BLOCK), BF16)] * 2
             for u in range(n):
-                source = jnp.broadcast_to(g_wide[u, pl.ds(pair * 2 + side, 1), :], (16, BLOCK))
-                first.append(pltpu.roll(source, 1, 1, stride=1, stride_axis=0).astype(BF16))
-            for k in range(BLOCK // 16):
-                other = jnp.zeros_like(first[0])
-                for u in range(n):
-                    turned = pltpu.roll(first[u], 16 * k, 1) if k else first[u]
-                    at = u * BLOCK + 16 * k
-                    toep[pair, at : at + 16, side * BLOCK : (side + 1) * BLOCK] = jnp.where(keep[k], turned, other)
-                    other = turned
-
-    def convolve(pair):
-        rows = []
-        for side in range(2):
-            at = (pair * 2 + side) * 2 * n + n
-            left = jnp.concatenate([h_pad[pl.ds(at - u, n), :] for u in range(n)], axis=1)
-            high = left.astype(BF16).astype(F32)
-            rows += [high, left - high]
-        both = jnp.concatenate(rows, axis=0).astype(BF16)
-        result = jnp.dot(both, toep[pair], preferred_element_type=F32)
-        y_tiles[rows_at(pair * 2 * n, n), :] = result[:n, :BLOCK] + result[n : 2 * n, :BLOCK]
-        y_tiles[rows_at(pair * 2 * n + n, n), :] = result[2 * n : 3 * n, BLOCK:] + result[3 * n :, BLOCK:]
-
-    def pairs(first, last):
+                source = jnp.broadcast_to(g_wide[u, pl.ds(group * GROUP + j, 1), :], (16, BLOCK))
+                first = pltpu.roll(source, 0, 1, stride=1, stride_axis=0).astype(BF16)
+                turned = [first, pltpu.roll(first, 16, 1)]
+                for k in range(2):
+                    at = 32 * j + 16 * k
+                    toep[group, at : at + 16, u * BLOCK : (u + 1) * BLOCK] = jnp.where(keep[k], turned[k], other[k])
+                other = turned
+
+    def correlate(left, group):
+        return lax.dot_general(left, toep[group], (((1,), (1,)), ((), ())), preferred_element_type=F32)
+
+    def put(tiles, group, result):
+        for j in range(GROUP):
+            half = j // 4 * BLOCK
+            tile = None
+            for r in range(4):
+                piece = result[32 * j + 8 * r : 32 * j + 8 * r + 8, half : half + BLOCK]
+                turn = 32 * (r - j % 4) % BLOCK
+                piece = pltpu.roll(piece, turn, 1) if turn else piece
+                tile = jnp.where(strip == r, piece, tile) if r else piece
+            tiles[rows_at(group * GROUP * n + j * n, n), :] = tile
+
+    def convolve(group):
+        result = correlate(h_left[group], group)
+        put(y_tiles, group, result[:256] + result[256:])
+
+    def groups(first, last):
         @pl.loop(first, last)
-        def _(pair):
-            convolve(pair - 1)
-            build(pair)
+        def _(group):
+            convolve(group - 1)
+            build(group)
 
     def add_block(at, block):
         if at:
@@ -307,9 +335,9 @@
 
         wide = grads.shape[2]
 
-        @pl.loop(0, 4)
+        @pl.loop(0, 2)
         def _(part):
-            size = acc.shape[0] // 4
+            size = acc.shape[0] // 2
             here = rows_at(part * size, size)
             term = lax.dot_general(
                 weight[here, rows_at(block * wide, wide)], grads[block],
@@ -319,15 +347,15 @@
 
     forward(1)
     build(0)
-    pairs(1, 16)
+    groups(1, 4)
     forward(2)
-    pairs(16, 32)
+    groups(4, 8)
     forward(3)
     weight_load.wait()
     own_grad.wait()
     add_block(0, c)
     add_block(1, partner)
-    pairs(32, 44)
+    groups(8, 11)
     add_block(2, near)
     add_block(3, far)
     for r in range(1, n + 1):
@@ -339,32 +367,39 @@
             exchange(d_send, d_recv, d_ssem, d_rsem, r).start()
         else:
             d_recv[me] = value
-    pairs(44, BLOCK // 2)
-    convolve(BLOCK // 2 - 1)
+    groups(11, BLOCK // GROUP)
+    convolve(BLOCK // GROUP - 1)
 
     for u in range(n):
-        y_send[u] = y_tiles[pl.ds(u, BLOCK, stride=n), :].astype(BF16)
+        y_send[u] = y_tiles[pl.ds(n - 1 - u, BLOCK, stride=n), :].astype(BF16)
     for r in range(1, n):
         exchange(y_send, y_recv, y_ssem, y_rsem, r).start()
     y_recv[me] = y_send[me]
 
     for r in range(1, n):
         exchange(d_send, d_recv, d_ssem, d_rsem, r).wait_recv()
-    for u in range(n):
-        d_pad[pl.ds(u, BLOCK, stride=2 * n), :] = d_recv[u].astype(F32)
-
-    @pl.loop(0, BLOCK // 4)
+    lay_out(d_pad, [d_recv[u].astype(F32) for u in range(n)])
+
+    def fill(left, group):
+        for j in range(GROUP):
+            for r in (0, 2):
+                for u in range(n):
+                    at = 32 * j + 8 * r
+                    value = left_rows(d_pad, group * GROUP + j, r, u)
+                    left[at : at + 16, u * BLOCK : (u + 1) * BLOCK] = value.astype(BF16)
+
+    last = BLOCK // GROUP - 1
+    fill(d_even, 0)
+
+    @pl.loop(0, BLOCK // GROUP // 2)
     def _(two):
-        for i in range(2):
-            pair = two * 2 + i
-            rows = []
-            for side in range(2):
-                at = (pair * 2 + side) * 2 * n
-                rows.append(jnp.concatenate([d_pad[pl.ds(at + u, n), :] for u in range(n)], axis=1))
-            both = jnp.concatenate(rows, axis=0).astype(BF16)
-            result = jnp.dot(both, toep[pair], preferred_element_type=F32)
-            f_tiles[rows_at(pair * 2 * n, n), :] = result[:n, :BLOCK]
-            f_tiles[rows_at(pair * 2 * n + n, n), :] = result[n:, BLOCK:]
+        group = two * 2
+        result = correlate(d_even[...], group)
+        fill(d_odd, group + 1)
+        put(f_tiles, group, result)
+        result = correlate(d_odd[...], group + 1)
+        fill(d_even, jnp.minimum(group + 2, last))
+        put(f_tiles, group + 1, result)
 
     for s in range(n):
         fgrad_ref[0, :, s * BLOCK : (s + 1) * BLOCK] = f_tiles[pl.ds(s, BLOCK, stride=n), :]
@@ -427,15 +462,18 @@
             pltpu.VMEM(blocks, BF16),
             pltpu.VMEM(blocks, BF16),
             pltpu.VMEM(blocks, F32),
-            pltpu.VMEM((channels // 2, length, 2 * BLOCK), BF16),
-            pltpu.VMEM((channels * 2 * n, BLOCK), F32),
+            pltpu.VMEM((channels // GROUP, 32 * GROUP, length), BF16),
+            pltpu.VMEM((4, channels * 2 * n, BLOCK), F32),
+            pltpu.VMEM((channels // GROUP, 64 * GROUP, length), BF16),
             pltpu.VMEM((channels * n, BLOCK), F32),
             pltpu.VMEM(blocks, BF16),
             pltpu.VMEM(blocks, BF16),
             pltpu.VMEM((group_w, tokens), F32),
             pltpu.VMEM(blocks, BF16),
             pltpu.VMEM(blocks, BF16),
-            pltpu.VMEM((channels * 2 * n, BLOCK), F32),
+            pltpu.VMEM((4, channels * 2 * n, BLOCK), F32),
+            pltpu.VMEM((32 * GROUP, length), BF16),
+            pltpu.VMEM((32 * GROUP, length), BF16),
             pltpu.VMEM((channels * n, BLOCK), F32),
             dma((6 + n,)),
             dma((3,)),

time: 56 us -> 45.8 us (0.82)
  Pallas kernels: 51.6 us -> 41.4 us
    pallas_call x1, Pallas kernels: 51.6 us -> 41.4 us  [on_device(): pl.pallas_call(kernel, out_shape=(jax.ShapeDtypeStruct(q_in.shape, BF16),...]
where the time goes in v2:
time: 45.8 us; the launch traced here: 45.6 us
  Pallas kernels  41.4 us (90%)
  local copies, waits for them, and re-layouts  3.55 us (8%)
  between operations  0.64 us (1%)
    pallas_call x1, Pallas kernels, on_device(): pl.pallas_call(kernel, out_shape=(jax.ShapeDtypeStruct(q_in.shape, BF16),...  41.4 us
    unnamed x2, local copies, waits for them, and re-layouts  3.55 us

profile of v2, /device:TPU:0, one launch (start us, length us, event | category | flops | bytes accessed | tf_op | source)
XLA Modules:
  0.0 45.6 jit_solution(11171205836638199399)
XLA Ops:
  0.6 41.4 %shard_map.86 = (bf16[128,1024]{1,0:T(8,128)(2,1)}, f32[1,128,1024]{2,1,0:T(8,128)}) custom-call(bf16[128,1024]{1,0:T(8,128)(2,1)} %q_hbm.1, bf16[128,1024]{1,0:T(8,128)(2,1)} %k_hbm.1, bf16[128,1024]{1,0:T(8,128)(2,1)} %v_hbm.1, f32[3,3,1024]{2,1,0:T(4,128)} %taps_hbm.1, f32[1,128,1024]{2,1,0:T(8,128)} %filt_hbm.1, bf16[1024,4096]{1,0:T(8,128)(2,1)} %weight_hbm.1, ...), custom_call_target="tpu_custom_call" | custom-call | tf_op jit(solution)/shard_map/pallas_call | solution.py:446
  42.1 1.7 %copy.11 = bf16[128,1024]{1,0:T(8,128)(2,1)} copy(bf16[128,1024]{1,0:T(8,128)(2,1)} %get-tuple-element.4) | data formatting | bytes 524288
  43.7 1.9 %copy.12 = f32[1,128,1024]{2,1,0:T(8,128)} copy(f32[1,128,1024]{2,1,0:T(8,128)} %get-tuple-element.5) | data formatting | bytes 1048576

commit v3 on v2

--- a/solution.py
+++ b/solution.py
@@ -122,8 +122,8 @@
     q_hbm, k_hbm, v_hbm, taps_hbm, filt_hbm, weight_hbm, grad_hbm,
     out_ref, fgrad_ref,
     streams, halo, taps, filt, weight, grads,
-    q_t, g_send, g_recv, g_wide, toep, h_pad, h_left, y_tiles, y_send, y_recv,
-    acc, d_send, d_recv, d_pad, d_even, d_odd, f_tiles,
+    q_t, g_send, g_recv, g_wide, toep, h_rev, y_tiles, y_send, y_recv,
+    acc, d_send, d_recv, fold, left_even, left_odd,
     load_sem, halo_ssem, halo_rsem, gather_ssem, gather_rsem, fwd_ssem,
     g_ssem, g_rsem, y_ssem, y_rsem, d_ssem, d_rsem,
 ):
@@ -206,43 +206,39 @@
     lane = lax.broadcasted_iota(jnp.int32, (BLOCK, BLOCK), 1)
     flip = jnp.where(row + lane == BLOCK - 1, 1.0, 0.0).astype(BF16)
 
-    def lay_out(pad, blocks):
-        pad[...] = jnp.zeros_like(pad)
+    def advance(tiles):
+        pairs = []
+        lane8 = lane[:8]
         for r in range(4):
-            turned = [pltpu.roll(x, BLOCK - 32 * r, 1) if r else x for x in blocks]
-            for a in range(n):
-                value = turned[a]
-                if r:
-                    after = turned[a + 1] if a + 1 < n else jnp.zeros_like(value)
-                    value = jnp.where(lane < BLOCK - 32 * r, value, after)
-                pad[r, pl.ds(a, BLOCK, stride=2 * n), :] = value
-
-    def left_rows(pad, channel, r, u):
-        at = channel * 2 * n
-        return jnp.concatenate([pad[r, pl.ds(at + u, n), :], pad[r + 1, pl.ds(at + u, n), :]], axis=0)
-
-    blocks = []
-    for a in reversed(range(n)):
+            turned = [pltpu.roll(x, BLOCK - 32 * r, 1) if r else x for x in tiles]
+            if r:
+                after = turned[1:] + [jnp.zeros_like(turned[0])]
+                turned = [jnp.where(lane8 < BLOCK - 32 * r, x, y) for x, y in zip(turned, after)]
+            turned.append(jnp.zeros_like(turned[0]))
+            pairs.append([jnp.concatenate(turned[v : v + 2], axis=0) for v in range(n)])
+        return pairs
+
+    def fill(left, first_row, pairs):
+        for r in range(4):
+            for v in range(n):
+                value = pairs[r][v].astype(BF16)
+                for m in range(v // 2 + 1):
+                    at = first_row + (m * 4 + r) * 16
+                    left[at : at + 16, (v - 2 * m) * BLOCK : (v - 2 * m + 1) * BLOCK] = value
+
+    left_even[...] = jnp.zeros_like(left_even)
+    left_odd[...] = jnp.zeros_like(left_odd)
+    size = fold.shape[0]
+    fold_row = lax.broadcasted_iota(jnp.int32, (size, BLOCK), 0) // GROUP
+    fold[...] = jnp.where(fold_row == lax.broadcasted_iota(jnp.int32, (size, BLOCK), 1), 1.0, 0.0).astype(BF16)
+
+    for a in range(n):
         filt_loads[a].wait()
         value = filt[a]
         high = value.astype(BF16)
         low = (value - high.astype(F32)).astype(BF16)
-        blocks.append(
-            jnp.dot(high, flip, preferred_element_type=F32) + jnp.dot(low, flip, preferred_element_type=F32)
-        )
-    lay_out(h_pad, blocks)
-
-    @pl.loop(0, BLOCK // GROUP)
-    def _(group):
-        for j in range(GROUP):
-            for r in (0, 2):
-                for u in range(n):
-                    value = left_rows(h_pad, group * GROUP + j, r, u)
-                    high = value.astype(BF16)
-                    at = 32 * j + 8 * r
-                    here = slice(u * BLOCK, (u + 1) * BLOCK)
-                    h_left[group, at : at + 16, here] = high
-                    h_left[group, 256 + at : 256 + at + 16, here] = (value - high.astype(F32)).astype(BF16)
+        turned = jnp.dot(high, flip, preferred_element_type=F32) + jnp.dot(low, flip, preferred_element_type=F32)
+        h_rev[n - 1 - a] = turned
 
     for copy in loads:
         copy.wait()
@@ -280,51 +276,66 @@
         else:
             g_recv[me] = gated
 
-    forward(0)
-    for r in range(1, n):
-        exchange(g_send, g_recv, g_ssem, g_rsem, r).wait_recv()
-    g_wide[...] = g_recv[...].astype(F32)
-
     lane16 = lax.broadcasted_iota(jnp.int32, (16, BLOCK), 1)
-    row16 = lax.broadcasted_iota(jnp.int32, (16, BLOCK), 0)
-    keep = [lane16 >= row16 + 16 * k for k in range(2)]
-    strip = lax.broadcasted_iota(jnp.int32, (n, BLOCK), 1) // 32
+    late = lane16 - lax.broadcasted_iota(jnp.int32, (16, BLOCK), 0) // GROUP
 
     def build(group):
-        for j in range(GROUP):
-            other = [jnp.zeros((16, BLOCK), BF16)] * 2
+        pairs = []
+        for u in range(n):
+            value = g_wide[u, rows_at(group * GROUP, GROUP), :]
+            pairs.append(jnp.concatenate([value, pltpu.roll(value, 1, 1)], axis=0).astype(BF16))
+        for two in range(16):
+            keep = late >= 2 * two
+            other = jnp.zeros((16, BLOCK), BF16)
             for u in range(n):
-                source = jnp.broadcast_to(g_wide[u, pl.ds(group * GROUP + j, 1), :], (16, BLOCK))
-                first = pltpu.roll(source, 0, 1, stride=1, stride_axis=0).astype(BF16)
-                turned = [first, pltpu.roll(first, 16, 1)]
-                for k in range(2):
-                    at = 32 * j + 16 * k
-                    toep[group, at : at + 16, u * BLOCK : (u + 1) * BLOCK] = jnp.where(keep[k], turned[k], other[k])
+                turned = pltpu.roll(pairs[u], 2 * two, 1) if two else pairs[u]
+                toep[group, 16 * two : 16 * two + 16, u * BLOCK : (u + 1) * BLOCK] = jnp.where(keep, turned, other)
                 other = turned
 
     def correlate(left, group):
         return lax.dot_general(left, toep[group], (((1,), (1,)), ((), ())), preferred_element_type=F32)
 
-    def put(tiles, group, result):
-        for j in range(GROUP):
-            half = j // 4 * BLOCK
-            tile = None
+    shape = (16, 2 * BLOCK)
+    own = lax.broadcasted_iota(jnp.int32, shape, 0) % GROUP == lax.broadcasted_iota(jnp.int32, shape, 1) % GROUP
+
+    def gather_own(result):
+        highs, lows = [], []
+        for m in range(4):
+            high, low = [], []
             for r in range(4):
-                piece = result[32 * j + 8 * r : 32 * j + 8 * r + 8, half : half + BLOCK]
-                turn = 32 * (r - j % 4) % BLOCK
-                piece = pltpu.roll(piece, turn, 1) if turn else piece
-                tile = jnp.where(strip == r, piece, tile) if r else piece
-            tiles[rows_at(group * GROUP * n + j * n, n), :] = tile
-
-    def convolve(group):
-        result = correlate(h_left[group], group)
-        put(y_tiles, group, result[:256] + result[256:])
-
-    def groups(first, last):
-        @pl.loop(first, last)
-        def _(group):
-            convolve(group - 1)
-            build(group)
+                at = (m * 4 + r) * 16
+                value = jnp.where(own, result[at : at + 16], 0.0)
+                high.append(value.astype(BF16))
+                low.append((value - high[-1].astype(F32)).astype(BF16))
+            highs.append(jnp.concatenate(high, axis=1))
+            lows.append(jnp.concatenate(low, axis=1))
+        parts = jnp.concatenate(highs + lows, axis=0)
+        folded = jnp.dot(parts, fold[...], preferred_element_type=F32)
+        return folded[: 8 * n] + folded[8 * n :]
+
+    def fill_filter(left, group):
+        pairs = advance([h_rev[v, rows_at(group * GROUP, GROUP), :] for v in range(n)])
+        fill(left, 0, pairs)
+        fill(left, 256, [[x - x.astype(BF16).astype(F32) for x in row_of] for row_of in pairs])
+
+    def convolve(left, group):
+        result = correlate(left[...], group)
+        folded = gather_own(result[:256] + result[256:])
+        for s in range(n):
+            y_tiles[n - 1 - s, rows_at(group * GROUP, GROUP), :] = folded[s * GROUP : (s + 1) * GROUP]
+
+    last = BLOCK // GROUP - 1
+
+    def groups(first, end):
+        @pl.loop(first // 2, end // 2)
+        def _(two):
+            group = two * 2
+            convolve(left_even, group)
+            fill_filter(left_odd, group + 1)
+            build(group + 1)
+            convolve(left_odd, group + 1)
+            fill_filter(left_even, jnp.minimum(group + 2, last))
+            build(jnp.minimum(group + 2, last))
 
     def add_block(at, block):
         if at:
@@ -345,17 +356,23 @@
             )
             acc[here, :] = term if at == 0 else acc[here, :] + term
 
+    weight_load.wait()
+    own_grad.wait()
+    add_block(0, c)
+    fill_filter(left_even, 0)
+    forward(0)
+    for r in range(1, n):
+        exchange(g_send, g_recv, g_ssem, g_rsem, r).wait_recv()
+    g_wide[...] = g_recv[...].astype(F32)
+
     forward(1)
     build(0)
-    groups(1, 4)
+    groups(0, 4)
     forward(2)
     groups(4, 8)
     forward(3)
-    weight_load.wait()
-    own_grad.wait()
-    add_block(0, c)
     add_block(1, partner)
-    groups(8, 11)
+    groups(8, 12)
     add_block(2, near)
     add_block(3, far)
     for r in range(1, n + 1):
@@ -367,42 +384,36 @@
             exchange(d_send, d_recv, d_ssem, d_rsem, r).start()
         else:
             d_recv[me] = value
-    groups(11, BLOCK // GROUP)
-    convolve(BLOCK // GROUP - 1)
+    groups(12, BLOCK // GROUP)
 
     for u in range(n):
-        y_send[u] = y_tiles[pl.ds(n - 1 - u, BLOCK, stride=n), :].astype(BF16)
+        y_send[u] = y_tiles[u].astype(BF16)
     for r in range(1, n):
         exchange(y_send, y_recv, y_ssem, y_rsem, r).start()
     y_recv[me] = y_send[me]
 
     for r in range(1, n):
         exchange(d_send, d_recv, d_ssem, d_rsem, r).wait_recv()
-    lay_out(d_pad, [d_recv[u].astype(F32) for u in range(n)])
-
-    def fill(left, group):
-        for j in range(GROUP):
-            for r in (0, 2):
-                for u in range(n):
-                    at = 32 * j + 8 * r
-                    value = left_rows(d_pad, group * GROUP + j, r, u)
-                    left[at : at + 16, u * BLOCK : (u + 1) * BLOCK] = value.astype(BF16)
-
-    last = BLOCK // GROUP - 1
-    fill(d_even, 0)
+    def put(group, result):
+        folded = gather_own(result)
+        for s in range(n):
+            fgrad_ref[0, rows_at(group * GROUP, GROUP), s * BLOCK : (s + 1) * BLOCK] = folded[s * GROUP : (s + 1) * GROUP]
+
+    def both_tiles(two):
+        return [d_recv[v, rows_at(two * 16, 16), :].astype(F32) for v in range(n)]
+
+    half = slice(0, 256)
+    fill(left_even, 0, advance([x[:GROUP] for x in both_tiles(0)]))
 
     @pl.loop(0, BLOCK // GROUP // 2)
     def _(two):
         group = two * 2
-        result = correlate(d_even[...], group)
-        fill(d_odd, group + 1)
-        put(f_tiles, group, result)
-        result = correlate(d_odd[...], group + 1)
-        fill(d_even, jnp.minimum(group + 2, last))
-        put(f_tiles, group + 1, result)
-
-    for s in range(n):
-        fgrad_ref[0, :, s * BLOCK : (s + 1) * BLOCK] = f_tiles[pl.ds(s, BLOCK, stride=n), :]
+        result = correlate(left_even[half], group)
+        fill(left_odd, 0, advance([x[GROUP:] for x in both_tiles(two)]))
+        put(group, result)
+        result = correlate(left_odd[half], group + 1)
+        fill(left_even, 0, advance([x[:GROUP] for x in both_tiles(jnp.minimum(two + 1, last // 2))]))
+        put(group + 1, result)
 
     for r in range(1, n):
         exchange(y_send, y_recv, y_ssem, y_rsem, r).wait_recv()
@@ -463,18 +474,16 @@
             pltpu.VMEM(blocks, BF16),
             pltpu.VMEM(blocks, F32),
             pltpu.VMEM((channels // GROUP, 32 * GROUP, length), BF16),
-            pltpu.VMEM((4, channels * 2 * n, BLOCK), F32),
-            pltpu.VMEM((channels // GROUP, 64 * GROUP, length), BF16),
-            pltpu.VMEM((channels * n, BLOCK), F32),
+            pltpu.VMEM(blocks, F32),
+            pltpu.VMEM(blocks, F32),
             pltpu.VMEM(blocks, BF16),
             pltpu.VMEM(blocks, BF16),
             pltpu.VMEM((group_w, tokens), F32),
             pltpu.VMEM(blocks, BF16),
             pltpu.VMEM(blocks, BF16),
-            pltpu.VMEM((4, channels * 2 * n, BLOCK), F32),
-            pltpu.VMEM((32 * GROUP, length), BF16),
-            pltpu.VMEM((32 * GROUP, length), BF16),
-            pltpu.VMEM((channels * n, BLOCK), F32),
+            pltpu.VMEM((4 * 32 * GROUP, BLOCK), BF16),
+            pltpu.VMEM((64 * GROUP, length), BF16),
+            pltpu.VMEM((64 * GROUP, length), BF16),
             dma((6 + n,)),
             dma((3,)),
             dma((3,)),

time: 45.8 us -> 49.1 us (1.072)
  Pallas kernels: 41.4 us -> 44.7 us
    pallas_call x1, Pallas kernels: 41.4 us -> 44.7 us  [on_device(): pl.pallas_call(kernel, out_shape=(jax.ShapeDtypeStruct(q_in.shape, BF16),...]
where the time goes in v3:
time: 49.1 us; the launch traced here: 48.9 us
  Pallas kernels  44.7 us (91%)
  local copies, waits for them, and re-layouts  3.55 us (7%)
  between operations  0.64 us (1%)
    pallas_call x1, Pallas kernels, on_device(): pl.pallas_call(kernel, out_shape=(jax.ShapeDtypeStruct(q_in.shape, BF16),...  44.7 us
    unnamed x2, local copies, waits for them, and re-layouts  3.55 us

profile of v3, /device:TPU:0, one launch (start us, length us, event | category | flops | bytes accessed | tf_op | source)
XLA Modules:
  0.0 48.9 jit_solution(5358563746033743627)
XLA Ops:
  0.6 44.7 %shard_map.86 = (bf16[128,1024]{1,0:T(8,128)(2,1)}, f32[1,128,1024]{2,1,0:T(8,128)}) custom-call(bf16[128,1024]{1,0:T(8,128)(2,1)} %q_hbm.1, bf16[128,1024]{1,0:T(8,128)(2,1)} %k_hbm.1, bf16[128,1024]{1,0:T(8,128)(2,1)} %v_hbm.1, f32[3,3,1024]{2,1,0:T(4,128)} %taps_hbm.1, f32[1,128,1024]{2,1,0:T(8,128)} %filt_hbm.1, bf16[1024,4096]{1,0:T(8,128)(2,1)} %weight_hbm.1, ...), custom_call_target="tpu_custom_call" | custom-call | tf_op jit(solution)/shard_map/pallas_call | solution.py:457
  45.3 1.7 %copy.11 = bf16[128,1024]{1,0:T(8,128)(2,1)} copy(bf16[128,1024]{1,0:T(8,128)(2,1)} %get-tuple-element.4) | data formatting | bytes 524288
  47.0 1.9 %copy.12 = f32[1,128,1024]{2,1,0:T(8,128)} copy(f32[1,128,1024]{2,1,0:T(8,128)} %get-tuple-element.5) | data formatting | bytes 1048576

commit v4 on v3

--- a/solution.py
+++ b/solution.py
@@ -123,7 +123,7 @@
     out_ref, fgrad_ref,
     streams, halo, taps, filt, weight, grads,
     q_t, g_send, g_recv, g_wide, toep, h_rev, y_tiles, y_send, y_recv,
-    acc, d_send, d_recv, fold, left_even, left_odd,
+    acc, d_send, d_recv, left_even, left_odd,
     load_sem, halo_ssem, halo_rsem, gather_ssem, gather_rsem, fwd_ssem,
     g_ssem, g_rsem, y_ssem, y_rsem, d_ssem, d_rsem,
 ):
@@ -228,9 +228,6 @@
 
     left_even[...] = jnp.zeros_like(left_even)
     left_odd[...] = jnp.zeros_like(left_odd)
-    size = fold.shape[0]
-    fold_row = lax.broadcasted_iota(jnp.int32, (size, BLOCK), 0) // GROUP
-    fold[...] = jnp.where(fold_row == lax.broadcasted_iota(jnp.int32, (size, BLOCK), 1), 1.0, 0.0).astype(BF16)
 
     for a in range(n):
         filt_loads[a].wait()
@@ -277,41 +274,44 @@
             g_recv[me] = gated
 
     lane16 = lax.broadcasted_iota(jnp.int32, (16, BLOCK), 1)
-    late = lane16 - lax.broadcasted_iota(jnp.int32, (16, BLOCK), 0) // GROUP
+    row16 = lax.broadcasted_iota(jnp.int32, (16, BLOCK), 0)
+    keep = [lane16 >= row16 + 16 * k for k in range(2)]
 
     def build(group):
-        pairs = []
-        for u in range(n):
-            value = g_wide[u, rows_at(group * GROUP, GROUP), :]
-            pairs.append(jnp.concatenate([value, pltpu.roll(value, 1, 1)], axis=0).astype(BF16))
-        for two in range(16):
-            keep = late >= 2 * two
-            other = jnp.zeros((16, BLOCK), BF16)
+        for j in range(GROUP):
+            other = [jnp.zeros((16, BLOCK), BF16)] * 2
             for u in range(n):
-                turned = pltpu.roll(pairs[u], 2 * two, 1) if two else pairs[u]
-                toep[group, 16 * two : 16 * two + 16, u * BLOCK : (u + 1) * BLOCK] = jnp.where(keep, turned, other)
+                source = jnp.broadcast_to(g_wide[u, pl.ds(group * GROUP + j, 1), :], (16, BLOCK))
+                first = pltpu.roll(source, 0, 1, stride=1, stride_axis=0).astype(BF16)
+                turned = [first, pltpu.roll(first, 16, 1)]
+                for k in range(2):
+                    at = 32 * j + 16 * k
+                    toep[group, at : at + 16, u * BLOCK : (u + 1) * BLOCK] = jnp.where(keep[k], turned[k], other[k])
                 other = turned
 
     def correlate(left, group):
         return lax.dot_general(left, toep[group], (((1,), (1,)), ((), ())), preferred_element_type=F32)
 
-    shape = (16, 2 * BLOCK)
-    own = lax.broadcasted_iota(jnp.int32, shape, 0) % GROUP == lax.broadcasted_iota(jnp.int32, shape, 1) % GROUP
+    low_half = row[:n] < 4
+    place = row[:n] % 4
+    strip = lane[:n] // 32
 
     def gather_own(result):
-        highs, lows = [], []
-        for m in range(4):
-            high, low = [], []
+        tiles = []
+        for s in range(n):
+            pieces = []
             for r in range(4):
-                at = (m * 4 + r) * 16
-                value = jnp.where(own, result[at : at + 16], 0.0)
-                high.append(value.astype(BF16))
-                low.append((value - high[-1].astype(F32)).astype(BF16))
-            highs.append(jnp.concatenate(high, axis=1))
-            lows.append(jnp.concatenate(low, axis=1))
-        parts = jnp.concatenate(highs + lows, axis=0)
-        folded = jnp.dot(parts, fold[...], preferred_element_type=F32)
-        return folded[: 8 * n] + folded[8 * n :]
+                at = ((s // 2 * 4 + r) * 2 + s % 2) * GROUP
+                pieces.append(jnp.where(low_half, result[at : at + GROUP, :BLOCK], result[at : at + GROUP, BLOCK:]))
+            tile = None
+            for q in range(4):
+                mixed = pieces[3]
+                for r in range(3):
+                    mixed = jnp.where(place == (r - q) % 4, pieces[r], mixed)
+                mixed = pltpu.roll(mixed, 32 * q, 1) if q else mixed
+                tile = jnp.where(strip == (place + q) % 4, mixed, tile) if q else mixed
+            tiles.append(tile)
+        return tiles
 
     def fill_filter(left, group):
         pairs = advance([h_rev[v, rows_at(group * GROUP, GROUP), :] for v in range(n)])
@@ -322,7 +322,7 @@
         result = correlate(left[...], group)
         folded = gather_own(result[:256] + result[256:])
         for s in range(n):
-            y_tiles[n - 1 - s, rows_at(group * GROUP, GROUP), :] = folded[s * GROUP : (s + 1) * GROUP]
+            y_tiles[n - 1 - s, rows_at(group * GROUP, GROUP), :] = folded[s]
 
     last = BLOCK // GROUP - 1
 
@@ -337,44 +337,57 @@
             fill_filter(left_even, jnp.minimum(group + 2, last))
             build(jnp.minimum(group + 2, last))
 
-    def add_block(at, block):
-        if at:
-            @pl.when(jnp.logical_or(jnp.logical_not(middle), at == 1))
-            def _():
-                for chunk in range(CHUNKS):
-                    gather_copy(block, chunk, grad_hbm.at[:, pl.ds(chunk * cols, cols)], partner, gather_ssem.at[0, chunk]).wait_recv()
-
-        wide = grads.shape[2]
+    half_cols = 2 * cols
+
+    def add_half(block, half, start):
+        at = rows_at(half * half_cols, half_cols)
+        size = acc.shape[0] // 2
 
         @pl.loop(0, 2)
         def _(part):
-            size = acc.shape[0] // 2
             here = rows_at(part * size, size)
             term = lax.dot_general(
-                weight[here, rows_at(block * wide, wide)], grads[block],
+                weight[here, rows_at(block * grads.shape[2] + half * half_cols, half_cols)], grads[block, :, at],
                 (((1,), (1,)), ((), ())), preferred_element_type=F32,
             )
-            acc[here, :] = term if at == 0 else acc[here, :] + term
+            acc[here, :] = term if start else acc[here, :] + term
+
+    def arrived(block, half):
+        for chunk in (2 * half, 2 * half + 1):
+            src = grad_hbm.at[:, pl.ds(chunk * cols, cols)]
+            gather_copy(block, chunk, src, partner, gather_ssem.at[0, chunk]).wait_recv()
+
+    def others_arrived(half):
+        @pl.when(jnp.logical_not(middle))
+        def _():
+            arrived(near, half)
+            arrived(far, half)
+
+        add_half(near, half, False)
+        add_half(far, half, False)
 
     weight_load.wait()
     own_grad.wait()
-    add_block(0, c)
+    add_half(c, 0, True)
+    add_half(c, 1, False)
+    forward(0)
     fill_filter(left_even, 0)
-    forward(0)
+    forward(1)
     for r in range(1, n):
         exchange(g_send, g_recv, g_ssem, g_rsem, r).wait_recv()
     g_wide[...] = g_recv[...].astype(F32)
 
-    forward(1)
     build(0)
+    forward(2)
     groups(0, 4)
-    forward(2)
+    forward(3)
+    for half in range(2):
+        arrived(partner, half)
+        add_half(partner, half, False)
     groups(4, 8)
-    forward(3)
-    add_block(1, partner)
-    groups(8, 12)
-    add_block(2, near)
-    add_block(3, far)
+    others_arrived(0)
+    groups(8, 10)
+    others_arrived(1)
     for r in range(1, n + 1):
         p = lax.rem(me + r, n)
         here = rows_at(p * BLOCK, BLOCK)
@@ -384,7 +397,7 @@
             exchange(d_send, d_recv, d_ssem, d_rsem, r).start()
         else:
             d_recv[me] = value
-    groups(12, BLOCK // GROUP)
+    groups(10, BLOCK // GROUP)
 
     for u in range(n):
         y_send[u] = y_tiles[u].astype(BF16)
@@ -397,7 +410,7 @@
     def put(group, result):
         folded = gather_own(result)
         for s in range(n):
-            fgrad_ref[0, rows_at(group * GROUP, GROUP), s * BLOCK : (s + 1) * BLOCK] = folded[s * GROUP : (s + 1) * GROUP]
+            fgrad_ref[0, rows_at(group * GROUP, GROUP), s * BLOCK : (s + 1) * BLOCK] = folded[s]
 
     def both_tiles(two):
         return [d_recv[v, rows_at(two * 16, 16), :].astype(F32) for v in range(n)]
@@ -481,7 +494,6 @@
             pltpu.VMEM((group_w, tokens), F32),
             pltpu.VMEM(blocks, BF16),
             pltpu.VMEM(blocks, BF16),
-            pltpu.VMEM((4 * 32 * GROUP, BLOCK), BF16),
             pltpu.VMEM((64 * GROUP, length), BF16),
             pltpu.VMEM((64 * GROUP, length), BF16),
             dma((6 + n,)),

time: 49.1 us -> 52.4 us (1.067)
  the two profiles are of different devices: /device:TPU:0 before, /device:TPU:8 now
where the time goes in v4:
time: 52.4 us; the launch traced here: 52.2 us
  Pallas kernels  48 us (92%)
  local copies, waits for them, and re-layouts  3.55 us (7%)
  between operations  0.64 us (1%)
    pallas_call x1, Pallas kernels, on_device(): pl.pallas_call(kernel, out_shape=(jax.ShapeDtypeStruct(q_in.shape, BF16),...  48 us
    unnamed x2, local copies, waits for them, and re-layouts  3.55 us

profile of v4, /device:TPU:8, one launch (start us, length us, event | category | flops | bytes accessed | tf_op | source)
XLA Modules:
  0.0 52.2 jit_solution(15726218731606777808)
XLA Ops:
  0.6 48.0 %shard_map.86 = (bf16[128,1024]{1,0:T(8,128)(2,1)}, f32[1,128,1024]{2,1,0:T(8,128)}) custom-call(bf16[128,1024]{1,0:T(8,128)(2,1)} %q_hbm.1, bf16[128,1024]{1,0:T(8,128)(2,1)} %k_hbm.1, bf16[128,1024]{1,0:T(8,128)(2,1)} %v_hbm.1, f32[3,3,1024]{2,1,0:T(4,128)} %taps_hbm.1, f32[1,128,1024]{2,1,0:T(8,128)} %filt_hbm.1, bf16[1024,4096]{1,0:T(8,128)(2,1)} %weight_hbm.1, ...), custom_call_target="tpu_custom_call" | custom-call | tf_op jit(solution)/shard_map/pallas_call | solution.py:470
  48.6 1.7 %copy.11 = bf16[128,1024]{1,0:T(8,128)(2,1)} copy(bf16[128,1024]{1,0:T(8,128)(2,1)} %get-tuple-element.4) | data formatting | bytes 524288
  50.3 1.9 %copy.12 = f32[1,128,1024]{2,1,0:T(8,128)} copy(f32[1,128,1024]{2,1,0:T(8,128)} %get-tuple-element.5) | data formatting | bytes 1048576

commit v5 on v2

--- a/solution.py
+++ b/solution.py
@@ -207,7 +207,6 @@
     flip = jnp.where(row + lane == BLOCK - 1, 1.0, 0.0).astype(BF16)
 
     def lay_out(pad, blocks):
-        pad[...] = jnp.zeros_like(pad)
         for r in range(4):
             turned = [pltpu.roll(x, BLOCK - 32 * r, 1) if r else x for x in blocks]
             for a in range(n):
@@ -221,28 +220,8 @@
         at = channel * 2 * n
         return jnp.concatenate([pad[r, pl.ds(at + u, n), :], pad[r + 1, pl.ds(at + u, n), :]], axis=0)
 
-    blocks = []
-    for a in reversed(range(n)):
-        filt_loads[a].wait()
-        value = filt[a]
-        high = value.astype(BF16)
-        low = (value - high.astype(F32)).astype(BF16)
-        blocks.append(
-            jnp.dot(high, flip, preferred_element_type=F32) + jnp.dot(low, flip, preferred_element_type=F32)
-        )
-    lay_out(h_pad, blocks)
-
-    @pl.loop(0, BLOCK // GROUP)
-    def _(group):
-        for j in range(GROUP):
-            for r in (0, 2):
-                for u in range(n):
-                    value = left_rows(h_pad, group * GROUP + j, r, u)
-                    high = value.astype(BF16)
-                    at = 32 * j + 8 * r
-                    here = slice(u * BLOCK, (u + 1) * BLOCK)
-                    h_left[group, at : at + 16, here] = high
-                    h_left[group, 256 + at : 256 + at + 16, here] = (value - high.astype(F32)).astype(BF16)
+    h_pad[...] = jnp.zeros_like(h_pad)
+    d_pad[...] = jnp.zeros_like(d_pad)
 
     for copy in loads:
         copy.wait()
@@ -280,7 +259,47 @@
         else:
             g_recv[me] = gated
 
+    blocks = []
+    for a in reversed(range(n)):
+        filt_loads[a].wait()
+        blocks.append(jnp.dot(filt[a].astype(BF16), flip, preferred_element_type=F32))
+    lay_out(h_pad, blocks)
+
+    def fill(left, pad, group):
+        for j in range(GROUP):
+            for r in (0, 2):
+                for u in range(n):
+                    at = 32 * j + 8 * r
+                    value = left_rows(pad, group * GROUP + j, r, u)
+                    left[at : at + 16, u * BLOCK : (u + 1) * BLOCK] = value.astype(BF16)
+
+    @pl.loop(0, BLOCK // GROUP)
+    def _(group):
+        fill(h_left.at[group], h_pad, group)
+
+    def add_block(at, block):
+        if at:
+            @pl.when(jnp.logical_or(jnp.logical_not(middle), at == 1))
+            def _():
+                for chunk in range(CHUNKS):
+                    gather_copy(block, chunk, grad_hbm.at[:, pl.ds(chunk * cols, cols)], partner, gather_ssem.at[0, chunk]).wait_recv()
+
+        wide = grads.shape[2]
+
+        @pl.loop(0, 2)
+        def _(part):
+            size = acc.shape[0] // 2
+            here = rows_at(part * size, size)
+            term = lax.dot_general(
+                weight[here, rows_at(block * wide, wide)], grads[block],
+                (((1,), (1,)), ((), ())), preferred_element_type=F32,
+            )
+            acc[here, :] = term if at == 0 else acc[here, :] + term
+
     forward(0)
+    weight_load.wait()
+    own_grad.wait()
+    add_block(0, c)
     for r in range(1, n):
         exchange(g_send, g_recv, g_ssem, g_rsem, r).wait_recv()
     g_wide[...] = g_recv[...].astype(F32)
@@ -317,8 +336,7 @@
             tiles[rows_at(group * GROUP * n + j * n, n), :] = tile
 
     def convolve(group):
-        result = correlate(h_left[group], group)
-        put(y_tiles, group, result[:256] + result[256:])
+        put(y_tiles, group, correlate(h_left[group], group))
 
     def groups(first, last):
         @pl.loop(first, last)
@@ -326,36 +344,14 @@
             convolve(group - 1)
             build(group)
 
-    def add_block(at, block):
-        if at:
-            @pl.when(jnp.logical_or(jnp.logical_not(middle), at == 1))
-            def _():
-                for chunk in range(CHUNKS):
-                    gather_copy(block, chunk, grad_hbm.at[:, pl.ds(chunk * cols, cols)], partner, gather_ssem.at[0, chunk]).wait_recv()
-
-        wide = grads.shape[2]
-
-        @pl.loop(0, 2)
-        def _(part):
-            size = acc.shape[0] // 2
-            here = rows_at(part * size, size)
-            term = lax.dot_general(
-                weight[here, rows_at(block * wide, wide)], grads[block],
-                (((1,), (1,)), ((), ())), preferred_element_type=F32,
-            )
-            acc[here, :] = term if at == 0 else acc[here, :] + term
-
     forward(1)
     build(0)
-    groups(1, 4)
+    groups(1, 3)
     forward(2)
-    groups(4, 8)
+    groups(3, 6)
     forward(3)
-    weight_load.wait()
-    own_grad.wait()
-    add_block(0, c)
     add_block(1, partner)
-    groups(8, 11)
+    groups(6, 10)
     add_block(2, near)
     add_block(3, far)
     for r in range(1, n + 1):
@@ -367,7 +363,7 @@
             exchange(d_send, d_recv, d_ssem, d_rsem, r).start()
         else:
             d_recv[me] = value
-    groups(11, BLOCK // GROUP)
+    groups(10, BLOCK // GROUP)
     convolve(BLOCK // GROUP - 1)
 
     for u in range(n):
@@ -380,25 +376,17 @@
         exchange(d_send, d_recv, d_ssem, d_rsem, r).wait_recv()
     lay_out(d_pad, [d_recv[u].astype(F32) for u in range(n)])
 
-    def fill(left, group):
-        for j in range(GROUP):
-            for r in (0, 2):
-                for u in range(n):
-                    at = 32 * j + 8 * r
-                    value = left_rows(d_pad, group * GROUP + j, r, u)
-                    left[at : at + 16, u * BLOCK : (u + 1) * BLOCK] = value.astype(BF16)
-
     last = BLOCK // GROUP - 1
-    fill(d_even, 0)
+    fill(d_even, d_pad, 0)
 
     @pl.loop(0, BLOCK // GROUP // 2)
     def _(two):
         group = two * 2
         result = correlate(d_even[...], group)
-        fill(d_odd, group + 1)
+        fill(d_odd, d_pad, group + 1)
         put(f_tiles, group, result)
         result = correlate(d_odd[...], group + 1)
-        fill(d_even, jnp.minimum(group + 2, last))
+        fill(d_even, d_pad, jnp.minimum(group + 2, last))
         put(f_tiles, group + 1, result)
 
     for s in range(n):
@@ -431,6 +419,18 @@
         exchange(g_send, g_recv, g_ssem, g_rsem, r).wait_send()
         exchange(y_send, y_recv, y_ssem, y_rsem, r).wait_send()
         exchange(d_send, d_recv, d_ssem, d_rsem, r).wait_send()
+
+
+def publish(out_in, fgrad_in, out_ref, fgrad_ref, sem):
+    copies = []
+    for i in range(4):
+        here = pl.ds(i * 32, 32)
+        copies.append(pltpu.make_async_copy(fgrad_in.at[:, here], fgrad_ref.at[:, here], sem.at[i]))
+        copies.append(pltpu.make_async_copy(out_in.at[here], out_ref.at[here], sem.at[4 + i]))
+    for copy in copies:
+        copy.start()
+    for copy in copies:
+        copy.wait()
 
 
 def on_device(q_in, k_in, v_in, short_filters, long_filter, out_weight, out_grad):
@@ -443,12 +443,10 @@
         return on_device_by_spectrum(q_in, k_in, v_in, short_filters, long_filter, out_weight, out_grad)
     dma = pltpu.SemaphoreType.DMA
     blocks = (n, BLOCK, BLOCK)
-    return pl.pallas_call(
+    shapes = (jax.ShapeDtypeStruct(q_in.shape, BF16), jax.ShapeDtypeStruct(long_filter.shape, F32))
+    results = pl.pallas_call(
         kernel,
-        out_shape=(
-            jax.ShapeDtypeStruct(q_in.shape, BF16),
-            jax.ShapeDtypeStruct(long_filter.shape, F32),
-        ),
+        out_shape=shapes,
         in_specs=[pl.BlockSpec(memory_space=pl.ANY)] * 7,
         out_specs=[pl.BlockSpec(memory_space=pltpu.VMEM)] * 2,
         scratch_shapes=[
@@ -464,7 +462,7 @@
             pltpu.VMEM(blocks, F32),
             pltpu.VMEM((channels // GROUP, 32 * GROUP, length), BF16),
             pltpu.VMEM((4, channels * 2 * n, BLOCK), F32),
-            pltpu.VMEM((channels // GROUP, 64 * GROUP, length), BF16),
+            pltpu.VMEM((channels // GROUP, 32 * GROUP, length), BF16),
             pltpu.VMEM((channels * n, BLOCK), F32),
             pltpu.VMEM(blocks, BF16),
             pltpu.VMEM(blocks, BF16),
@@ -492,6 +490,14 @@
             collective_id=0, has_side_effects=True, vmem_limit_bytes=60 * 1024 * 1024
         ),
     )(q_in, k_in, v_in, short_filters, long_filter, out_weight, out_grad)
+    return pl.pallas_call(
+        publish,
+        out_shape=shapes,
+        in_specs=[pl.BlockSpec(memory_space=pl.ANY)] * 2,
+        out_specs=[pl.BlockSpec(memory_space=pl.ANY)] * 2,
+        scratch_shapes=[dma((8,))],
+        compiler_params=pltpu.CompilerParams(vmem_limit_bytes=60 * 1024 * 1024),
+    )(*results)
 
 
 def solution(mesh):

time: 45.8 us -> 64.9 us (1.42)
  Pallas kernels: 41.4 us -> 64.1 us
  local copies, waits for them, and re-layouts: 3.55 us -> 0 us
    pallas_call x1 -> x2, Pallas kernels: 41.4 us -> 64.1 us  [the longest x1 39.1 us: on_device(): pl.pallas_call(kernel, out_shape=shapes, in_specs=[pl.BlockSpec(memory_sp...]
    unnamed x2 -> x0, local copies, waits for them, and re-layouts: 3.55 us -> none
where the time goes in v5:
time: 64.9 us; the launch traced here: 64.8 us
  Pallas kernels  64.1 us (99%)
    pallas_call x1, Pallas kernels, on_device(): pl.pallas_call(kernel, out_shape=shapes, in_specs=[pl.BlockSpec(memory_sp...  39.1 us
    pallas_call x1, Pallas kernels, on_device(): pl.pallas_call(publish, out_shape=shapes, in_specs=[pl.BlockSpec(memory_s...  25 us

profile of v5, /device:TPU:0, one launch (start us, length us, event | category | flops | bytes accessed | tf_op | source)
XLA Modules:
  0.0 64.8 jit_solution(8737343949918035863)
XLA Ops:
  0.6 39.1 %shard_map.86 = (bf16[128,1024]{1,0:T(8,128)(2,1)}, f32[1,128,1024]{2,1,0:T(8,128)}) custom-call(bf16[128,1024]{1,0:T(8,128)(2,1)} %q_hbm.1, bf16[128,1024]{1,0:T(8,128)(2,1)} %k_hbm.1, bf16[128,1024]{1,0:T(8,128)(2,1)} %v_hbm.1, f32[3,3,1024]{2,1,0:T(4,128)} %taps_hbm.1, f32[1,128,1024]{2,1,0:T(8,128)} %filt_hbm.1, bf16[1024,4096]{1,0:T(8,128)(2,1)} %weight_hbm.1, ...), custom_call_target="tpu_custom_call" | custom-call | tf_op jit(solution)/shard_map/pallas_call | solution.py:447
  39.8 25.0 %shard_map.87 = (bf16[128,1024]{1,0:T(8,128)(2,1)}, f32[1,128,1024]{2,1,0:T(8,128)}) custom-call(bf16[128,1024]{1,0:T(8,128)(2,1)} %get-tuple-element.4.out_in, f32[1,128,1024]{2,1,0:T(8,128)} %get-tuple-element.5.fgrad_in), custom_call_target="tpu_custom_call" | custom-call | tf_op jit(solution)/shard_map/pallas_call | solution.py:493

commit v6 on v5

--- a/solution.py
+++ b/solution.py
@@ -122,7 +122,7 @@
     q_hbm, k_hbm, v_hbm, taps_hbm, filt_hbm, weight_hbm, grad_hbm,
     out_ref, fgrad_ref,
     streams, halo, taps, filt, weight, grads,
-    q_t, g_send, g_recv, g_wide, toep, h_pad, h_left, y_tiles, y_send, y_recv,
+    q_t, g_send, g_recv, g_wide, turns, toep, h_pad, h_left, y_tiles, y_send, y_recv,
     acc, d_send, d_recv, d_pad, d_even, d_odd, f_tiles,
     load_sem, halo_ssem, halo_rsem, gather_ssem, gather_rsem, fwd_ssem,
     g_ssem, g_rsem, y_ssem, y_rsem, d_ssem, d_rsem,
@@ -310,11 +310,15 @@
     strip = lax.broadcasted_iota(jnp.int32, (n, BLOCK), 1) // 32
 
     def build(group):
+        for u in range(n):
+            value = g_wide[u, rows_at(group * GROUP, GROUP), :]
+            for delay in range(16):
+                turned = pltpu.roll(value, delay, 1) if delay else value
+                turns[pl.ds(u * BLOCK + delay, GROUP, stride=16), :] = turned
         for j in range(GROUP):
             other = [jnp.zeros((16, BLOCK), BF16)] * 2
             for u in range(n):
-                source = jnp.broadcast_to(g_wide[u, pl.ds(group * GROUP + j, 1), :], (16, BLOCK))
-                first = pltpu.roll(source, 0, 1, stride=1, stride_axis=0).astype(BF16)
+                first = turns[u * BLOCK + 16 * j : u * BLOCK + 16 * j + 16, :].astype(BF16)
                 turned = [first, pltpu.roll(first, 16, 1)]
                 for k in range(2):
                     at = 32 * j + 16 * k
@@ -421,15 +425,22 @@
         exchange(d_send, d_recv, d_ssem, d_rsem, r).wait_send()
 
 
-def publish(out_in, fgrad_in, out_ref, fgrad_ref, sem):
-    copies = []
+def publish(out_in, fgrad_in, out_ref, fgrad_ref, out_held, fgrad_held, load_sem, store_sem):
+    loads, stores = [], []
     for i in range(4):
         here = pl.ds(i * 32, 32)
-        copies.append(pltpu.make_async_copy(fgrad_in.at[:, here], fgrad_ref.at[:, here], sem.at[i]))
-        copies.append(pltpu.make_async_copy(out_in.at[here], out_ref.at[here], sem.at[4 + i]))
-    for copy in copies:
+        for at, (src, held, dst) in enumerate(
+            ((fgrad_in.at[0], fgrad_held, fgrad_ref.at[0]), (out_in, out_held, out_ref))
+        ):
+            k = 2 * i + at
+            loads.append(pltpu.make_async_copy(src.at[here], held.at[here], load_sem.at[k]))
+            stores.append(pltpu.make_async_copy(held.at[here], dst.at[here], store_sem.at[k]))
+    for copy in loads:
         copy.start()
-    for copy in copies:
+    for load, store in zip(loads, stores):
+        load.wait()
+        store.start()
+    for copy in stores:
         copy.wait()
 
 
@@ -460,6 +471,7 @@
             pltpu.VMEM(blocks, BF16),
             pltpu.VMEM(blocks, BF16),
             pltpu.VMEM(blocks, F32),
+            pltpu.VMEM((n * BLOCK, BLOCK), F32),
             pltpu.VMEM((channels // GROUP, 32 * GROUP, length), BF16),
             pltpu.VMEM((4, channels * 2 * n, BLOCK), F32),
             pltpu.VMEM((channels // GROUP, 32 * GROUP, length), BF16),
@@ -495,7 +507,12 @@
         out_shape=shapes,
         in_specs=[pl.BlockSpec(memory_space=pl.ANY)] * 2,
         out_specs=[pl.BlockSpec(memory_space=pl.ANY)] * 2,
-        scratch_shapes=[dma((8,))],
+        scratch_shapes=[
+            pltpu.VMEM(q_in.shape, BF16),
+            pltpu.VMEM(long_filter.shape[1:], F32),
+            dma((8,)),
+            dma((8,)),
+        ],
         compiler_params=pltpu.CompilerParams(vmem_limit_bytes=60 * 1024 * 1024),
     )(*results)
 

time: 64.9 us -> 41.9 us (0.65)
  Pallas kernels: 64.1 us -> 41.1 us
    pallas_call x1, Pallas kernels: 25 us -> 2 us  [on_device(): pl.pallas_call(publish, out_shape=shapes, in_specs=[pl.BlockSpec(memory_s...]
where the time goes in v6:
time: 41.9 us; the launch traced here: 41.8 us
  Pallas kernels  41.1 us (98%)
  between operations  0.64 us (2%)
    pallas_call x1, Pallas kernels, on_device(): pl.pallas_call(kernel, out_shape=shapes, in_specs=[pl.BlockSpec(memory_sp...  39.1 us
    pallas_call x1, Pallas kernels, on_device(): pl.pallas_call(publish, out_shape=shapes, in_specs=[pl.BlockSpec(memory_s...  2 us

profile of v6, /device:TPU:0, one launch (start us, length us, event | category | flops | bytes accessed | tf_op | source)
XLA Modules:
  0.0 41.8 jit_solution(17063658352612233102)
XLA Ops:
  0.6 39.1 %shard_map.86 = (bf16[128,1024]{1,0:T(8,128)(2,1)}, f32[1,128,1024]{2,1,0:T(8,128)}) custom-call(bf16[128,1024]{1,0:T(8,128)(2,1)} %q_hbm.1, bf16[128,1024]{1,0:T(8,128)(2,1)} %k_hbm.1, bf16[128,1024]{1,0:T(8,128)(2,1)} %v_hbm.1, f32[3,3,1024]{2,1,0:T(4,128)} %taps_hbm.1, f32[1,128,1024]{2,1,0:T(8,128)} %filt_hbm.1, bf16[1024,4096]{1,0:T(8,128)(2,1)} %weight_hbm.1, ...), custom_call_target="tpu_custom_call" | custom-call | tf_op jit(solution)/shard_map/pallas_call | solution.py:458
  39.8 2.0 %shard_map.87 = (bf16[128,1024]{1,0:T(8,128)(2,1)}, f32[1,128,1024]{2,1,0:T(8,128)}) custom-call(bf16[128,1024]{1,0:T(8,128)(2,1)} %get-tuple-element.4.out_in, f32[1,128,1024]{2,1,0:T(8,128)} %get-tuple-element.5.fgrad_in), custom_call_target="tpu_custom_call" | custom-call | tf_op jit(solution)/shard_map/pallas_call | solution.py:505

commit v7 on v6

--- a/solution.py
+++ b/solution.py
@@ -350,12 +350,12 @@
 
     forward(1)
     build(0)
-    groups(1, 3)
+    groups(1, 2)
     forward(2)
-    groups(3, 6)
+    groups(2, 4)
     forward(3)
     add_block(1, partner)
-    groups(6, 10)
+    groups(4, 10)
     add_block(2, near)
     add_block(3, far)
     for r in range(1, n + 1):

time: 41.9 us -> 41.9 us (level)
  no operation moved by 1% of the time
where the time goes in v7:
time: 41.9 us; the launch traced here: 41.8 us
  Pallas kernels  41.1 us (98%)
  between operations  0.64 us (2%)
    pallas_call x1, Pallas kernels, on_device(): pl.pallas_call(kernel, out_shape=shapes, in_specs=[pl.BlockSpec(memory_sp...  39.1 us
    pallas_call x1, Pallas kernels, on_device(): pl.pallas_call(publish, out_shape=shapes, in_specs=[pl.BlockSpec(memory_s...  2 us

profile of v7, /device:TPU:0, one launch (start us, length us, event | category | flops | bytes accessed | tf_op | source)
XLA Modules:
  0.0 41.8 jit_solution(10138719172583731081)
XLA Ops:
  0.6 39.1 %shard_map.86 = (bf16[128,1024]{1,0:T(8,128)(2,1)}, f32[1,128,1024]{2,1,0:T(8,128)}) custom-call(bf16[128,1024]{1,0:T(8,128)(2,1)} %q_hbm.1, bf16[128,1024]{1,0:T(8,128)(2,1)} %k_hbm.1, bf16[128,1024]{1,0:T(8,128)(2,1)} %v_hbm.1, f32[3,3,1024]{2,1,0:T(4,128)} %taps_hbm.1, f32[1,128,1024]{2,1,0:T(8,128)} %filt_hbm.1, bf16[1024,4096]{1,0:T(8,128)(2,1)} %weight_hbm.1, ...), custom_call_target="tpu_custom_call" | custom-call | tf_op jit(solution)/shard_map/pallas_call | solution.py:458
  39.8 2.0 %shard_map.87 = (bf16[128,1024]{1,0:T(8,128)(2,1)}, f32[1,128,1024]{2,1,0:T(8,128)}) custom-call(bf16[128,1024]{1,0:T(8,128)(2,1)} %get-tuple-element.4.out_in, f32[1,128,1024]{2,1,0:T(8,128)} %get-tuple-element.5.fgrad_in), custom_call_target="tpu_custom_call" | custom-call | tf_op jit(solution)/shard_map/pallas_call | solution.py:505
